TPU v7x, 512 devices: a whole 4x4x16 slice. The times are simulated.
512 devices in a mesh: dom: 64 (over x, z), sub: 8 (over y, core).
Axes of the slice: x: 4, y: 4, z: 16, core: 2. Of those that a mesh axis runs over, the one named last changes fastest.
Arguments:
- right_side: float32 [1024, 16, 128], P(('dom', 'sub')), as said below
- diag_blocks: float32 [1024, 128, 128], P(('dom', 'sub')), as said below
- block_values: float32 [1024, 4, 128, 128], P(('dom', 'sub')), as said below
- block_cols: int32 [1024, 4], P(('dom', 'sub')), may hold values from 0 to 31, as said below
- block_count: int32 [1024], P(('dom', 'sub')), may hold values from 0 to 4, as said below
- cell_diagonal: float32 [1024, 128], P(('dom', 'sub')), as said below
Outputs:
- solution_field: float32 [1024, 16, 128], P(('dom', 'sub'))
- residual: float32 [1024, 16, 128], P(('dom', 'sub'))
Inputs may be any that keep to these rules, and one draw needn't show every extreme that they name: `block_cols`: live slots of a block row point to distinct block rows that come after it in the window (positions 0 to 15 are the block rows of the same index of dom, the rest those of the next index); block rows of the last index of dom point only into their own index; dead slots hold 0. `block_count`: the number of live slots, which varies from device to device. `block_values`: entries lie between -1 / 128 and 0. `diag_blocks`: entries lie between -1 / 128 and 0. `cell_diagonal`: every entry exceeds 1 + the live slots of its block row + the live slots of all block rows that couple to its block row, so the operator is strictly diagonally dominant. `right_side`: entries lie between -50 and 50.
All inputs are finite; a program needn't handle non-finite values.
Results may differ from a plain program's by a relative error of at most 0.00065.
Values sent between devices are 32-bit elements; how exact they have to be, the bound alone decides.
A program may use at most 64 MiB of HBM per device.

v0:
```python
import jax
import jax.numpy as jnp
from jax import lax
from jax.sharding import PartitionSpec as P

K = 4
ITERS = 3
PRECISE = lax.Precision.HIGHEST


def passed_along(x, axis, by):
    peers = lax.axis_size(axis)
    pairs = [(i, i + by) for i in range(peers) if 0 <= i + by < peers]
    return lax.ppermute(x, axis, pairs)


def local(right_side, diag_blocks, block_values, block_cols, block_count, cell_diagonal):
    rows_dev = right_side.shape[0]
    group_rows = lax.axis_size("sub") * rows_dev
    upper_part = jnp.triu(diag_blocks, 1)
    live_slots = jnp.arange(K, dtype=jnp.int32)[None, :] < block_count[:, None]
    window_ids = jnp.arange(2 * group_rows, dtype=jnp.int32)
    picker = (
        (block_cols[:, :, None] == window_ids[None, None, :]) & live_slots[:, :, None]
    ).astype(jnp.float32)

    def local_dots(first, second):
        return jnp.sum(first * second, axis=(0, 2))

    def residual_sum(residual_now, precond_now):
        return lax.psum(local_dots(residual_now, precond_now), ("dom", "sub"))

    solution_field = jnp.zeros_like(right_side)
    residual = right_side
    precond_res = residual / cell_diagonal[:, None, :]
    direction = precond_res
    precond_dot = residual_sum(residual, precond_res)
    for iteration in range(ITERS):
        own_part = jnp.einsum("rab,rzb->rza", upper_part, direction, precision=PRECISE)
        own_part = own_part + jnp.einsum("rba,rzb->rza", upper_part, direction, precision=PRECISE)
        own_part = own_part + cell_diagonal[:, None, :] * direction
        own_group = lax.all_gather(direction, "sub", axis=0, tiled=True)
        next_group = passed_along(own_group, "dom", -1)
        window = jnp.concatenate([own_group, next_group], axis=0)
        far_rows = jnp.einsum("rkw,wzb->rkzb", picker, window, precision=PRECISE)
        forward = jnp.einsum("rkab,rkzb->rza", block_values, far_rows, precision=PRECISE)
        back_terms = jnp.einsum("rkba,rzb->rkza", block_values, direction, precision=PRECISE)
        spread = jnp.einsum("rkw,rkza->wza", picker, back_terms, precision=PRECISE)
        incoming = passed_along(spread[group_rows:], "dom", 1)
        back_own = lax.psum_scatter(
            spread[:group_rows] + incoming, "sub", scatter_dimension=0, tiled=True
        )
        image_vec = own_part + forward + back_own
        curvature = lax.psum(local_dots(direction, image_vec), ("dom", "sub"))
        step_size = precond_dot / curvature
        solution_field = solution_field + step_size[None, :, None] * direction
        residual = residual - step_size[None, :, None] * image_vec
        if iteration + 1 < ITERS:
            precond_res = residual / cell_diagonal[:, None, :]
            new_dot = residual_sum(residual, precond_res)
            direction = precond_res + (new_dot / precond_dot)[None, :, None] * direction
            precond_dot = new_dot
    return (solution_field, residual)


def solution(mesh):
    return jax.shard_map(
        local,
        mesh=mesh,
        in_specs=(
            P(("dom", "sub"), None, None),
            P(("dom", "sub"), None, None),
            P(("dom", "sub"), None, None, None),
            P(("dom", "sub"), None),
            P(("dom", "sub")),
            P(("dom", "sub"), None),
        ),
        out_specs=(P(("dom", "sub"), None, None), P(("dom", "sub"), None, None)),
        check_vma=False,
    )
```

profile of v0, /device:TPU:1, one launch (start us, length us, event | category | flops | bytes accessed | tf_op | source)
XLA Modules:
  0.0 715.4 jit_solution(11586665640421009732)
XLA Ops:
  7.2 0.8 broadcast_divide_fusion
  8.0 19.6 %all_gather.9 = f32[16,16,128]{2,1,0:T(8,128)S(1)} all-gather(f32[2,16,128]{2,1,0:T(8,128)S(1)} %broadcast_divide_fusion), channel_id=1, replica_groups=mesh['dom'=64,'sub'=8] {'sub'}, dimensions={0}, use_global_device_ids=true | all-gather | bytes 147456 | tf_op jit(solution)/shard_map/all_gather | solution.py:42
  27.6 1.4 collective-permute-start
  30.3 4.0 collective-permute-start.1
  35.0 1.7 collective-permute-done.1
  38.2 37.2 %reduce-scatter.4.cloned.1.call-done = f32[2,16,128]{2,1,0:T(8,128)} async-done(((f32[16,16,128]{2,1,0:T(8,128)}), f32[2,16,128]{2,1,0:T(8,128)}) %reduce-scatter.4.cloned.1.call-update) | async-done | bytes 16400 | tf_op jit(solution)/shard_map/reduce_scatter | solution.py:50
  75.4 0.8 multiply_reduce_fusion.4
  76.2 105.7 %all-reduce = (f32[16]{0:T(128)S(1)}, f32[16]{0:T(128)S(1)}) all-reduce(f32[16]{0:T(128)S(1)} %get-tuple-element.3, f32[16]{0:T(128)S(1)} %get-tuple-element.2), channel_id=1, replica_groups=mesh['dom'=64,'sub'=8] {'dom','sub'}, use_global_device_ids=true, to_apply=%region_1.2 | all-reduce | flops 32 | bytes 256 | tf_op jit(solution)/shard_map/psum | solution.py:31
  182.2 99.4 %psum.44 = f32[16]{0:T(128)S(1)} all-reduce(f32[16]{0:T(128)S(1)} %get-tuple-element.12), channel_id=1, replica_groups=mesh['dom'=64,'sub'=8] {'dom','sub'}, use_global_device_ids=true, to_apply=%region_6.7 | all-reduce | flops 16 | bytes 128 | tf_op jit(solution)/shard_map/psum | solution.py:31
  281.7 13.2 %all_gather.10 = f32[16,16,128]{2,1,0:T(8,128)S(1)} all-gather(f32[2,16,128]{2,1,0:T(8,128)S(1)} %multiply_add_fusion.2), channel_id=1, replica_groups=mesh['dom'=64,'sub'=8] {'sub'}, dimensions={0}, use_global_device_ids=true | all-gather | bytes 147456 | tf_op jit(solution)/shard_map/all_gather | solution.py:42
  295.3 1.3 collective-permute-start.2
  297.1 4.0 collective-permute-start.3
  302.4 1.0 collective-permute-done.3
  305.0 33.6 %reduce-scatter.6.cloned.1.call-done = f32[2,16,128]{2,1,0:T(8,128)} async-done(((f32[16,16,128]{2,1,0:T(8,128)}), f32[2,16,128]{2,1,0:T(8,128)}) %reduce-scatter.6.cloned.1.call-update) | async-done | bytes 16400 | tf_op jit(solution)/shard_map/reduce_scatter | solution.py:50
  338.5 0.8 multiply_reduce_fusion.2
  339.4 105.7 %psum.45 = f32[16]{0:T(128)S(1)} all-reduce(f32[16]{0:T(128)S(1)} %get-tuple-element.10), channel_id=1, replica_groups=mesh['dom'=64,'sub'=8] {'dom','sub'}, use_global_device_ids=true, to_apply=%region_9.10 | all-reduce | flops 16 | bytes 128 | tf_op jit(solution)/shard_map/psum | solution.py:54
  445.3 99.2 %psum.46 = f32[16]{0:T(128)S(1)} all-reduce(f32[16]{0:T(128)S(1)} %get-tuple-element.8), channel_id=1, replica_groups=mesh['dom'=64,'sub'=8] {'dom','sub'}, use_global_device_ids=true, to_apply=%region_11.12 | all-reduce | flops 16 | bytes 128 | tf_op jit(solution)/shard_map/psum | solution.py:31
  544.6 13.2 %all_gather.11 = f32[16,16,128]{2,1,0:T(8,128)S(1)} all-gather(f32[2,16,128]{2,1,0:T(8,128)S(1)} %multiply_add_fusion.1), channel_id=1, replica_groups=mesh['dom'=64,'sub'=8] {'sub'}, dimensions={0}, use_global_device_ids=true | all-gather | bytes 147456 | tf_op jit(solution)/shard_map/all_gather | solution.py:42
  558.2 1.3 collective-permute-start.4
  560.0 4.0 collective-permute-start.5
  565.3 1.0 collective-permute-done.5
  567.8 33.7 %reduce-scatter.8.cloned.1.call-done = f32[2,16,128]{2,1,0:T(8,128)} async-done(((f32[16,16,128]{2,1,0:T(8,128)}), f32[2,16,128]{2,1,0:T(8,128)}) %reduce-scatter.8.cloned.1.call-update) | async-done | bytes 16400 | tf_op jit(solution)/shard_map/reduce_scatter | solution.py:50
  601.5 0.8 multiply_reduce_fusion
  602.4 105.8 %psum.47 = f32[16]{0:T(128)S(1)} all-reduce(f32[16]{0:T(128)S(1)} %get-tuple-element.6), channel_id=1, replica_groups=mesh['dom'=64,'sub'=8] {'dom','sub'}, use_global_device_ids=true, to_apply=%region_14.15 | all-reduce | flops 16 | bytes 128 | tf_op jit(solution)/shard_map/psum | solution.py:54
  (63 shorter events, 11.9 us)
Async XLA Ops:
  7.2 21.9 %copy-start = (f32[2,4,128,128]{3,2,1,0:T(8,128)S(1)}, f32[2,4,128,128]{3,2,1,0:T(8,128)}, u32[]{:S(2)}) copy-start(f32[2,4,128,128]{3,2,1,0:T(8,128)} %param.8) | copy-start | bytes 1572868
  7.2 68.2 %reduce-scatter.4.cloned.1.call-start = ((), (), s32[]{:S(2)}) async-start(), calls=%async_computation.3 | async-start | bytes 147456 | tf_op jit(solution)/shard_map/reduce_scatter | solution.py:50
  8.0 21.0 %copy-start.5 = (s32[2]{0:T(128)S(1)}, s32[2]{0:T(128)}, u32[]{:S(2)}) copy-start(s32[2]{0:T(128)} %param.10) | copy-start | bytes 28
  8.0 21.1 %copy-start.2 = (f32[2,16,128]{2,1,0:T(8,128)S(1)}, f32[2,16,128]{2,1,0:T(8,128)}, u32[]{:S(2)}) copy-start(f32[2,16,128]{2,1,0:T(8,128)} %param.6) | copy-start | bytes 49156
  27.6 1.5 copy-start.3
  27.6 7.0 collective-permute-start
  29.1 0.7 copy-start.4
  30.2 4.1 copy-start.1
  30.3 6.4 collective-permute-start.1
  37.4 301.1 %reduce-scatter.6.cloned.1.call-start = ((), (), s32[]{:S(2)}) async-start(), calls=%async_computation.4 | async-start | bytes 147456 | tf_op jit(solution)/shard_map/reduce_scatter | solution.py:50
  295.3 6.8 collective-permute-start.2
  297.1 6.4 collective-permute-start.3
  304.2 297.4 %reduce-scatter.8.cloned.1.call-start = ((), (), s32[]{:S(2)}) async-start(), calls=%async_computation.5 | async-start | bytes 147456 | tf_op jit(solution)/shard_map/reduce_scatter | solution.py:50
  558.2 6.8 collective-permute-start.4
  560.0 6.4 collective-permute-start.5
Sparse Core Ops, SparseCore 0:
  37.5 37.8 reduce-scatter.3
  304.3 34.2 reduce-scatter.5
  567.2 34.3 reduce-scatter.7
where the time goes:
time: 717 us; the launch traced here: 715 us
  blocking collectives  562 us (78%)
  waiting for transfers between devices  110 us (15%)
  starting transfers between devices  16.1 us (2%)
  between operations  14 us (2%)
    psum x3, blocking collectives, residual_sum(): return lax.psum(local_dots(residual_now, precond_now), ('dom', 'sub'))  304 us
    psum x2, blocking collectives, local(): curvature = lax.psum(local_dots(direction, image_vec), ('dom', 'sub'))  212 us
    reduce_scatter x3, waiting for transfers between devices, local(): lax.psum_scatter(spread[:group_rows] + incoming, 'sub', scatter_dimension...  104 us
    all_gather x3, blocking collectives, local(): own_group = lax.all_gather(direction, 'sub', axis=0, tiled=True)  46.1 us
    ppermute x6, starting transfers between devices, passed_along(): return lax.ppermute(x, axis, pairs)  16 us
  transfers between devices with their start and end apart: 9, of which 8 were waited for; matrix products, arithmetic and copies ran while one was open for 1% of the time, Pallas kernels for 0%

commit v1 on v0

--- a/solution.py
+++ b/solution.py
@@ -39,7 +39,9 @@
         own_part = jnp.einsum("rab,rzb->rza", upper_part, direction, precision=PRECISE)
         own_part = own_part + jnp.einsum("rba,rzb->rza", upper_part, direction, precision=PRECISE)
         own_part = own_part + cell_diagonal[:, None, :] * direction
-        own_group = lax.all_gather(direction, "sub", axis=0, tiled=True)
+        own_group = jnp.concatenate(
+            lax.all_to_all(jnp.stack([direction] * lax.axis_size("sub")), "sub", 0, 0), axis=0
+        )
         next_group = passed_along(own_group, "dom", -1)
         window = jnp.concatenate([own_group, next_group], axis=0)
         far_rows = jnp.einsum("rkw,wzb->rkzb", picker, window, precision=PRECISE)

time: 717 us -> 689 us (0.961)
  blocking collectives: 562 us -> 516 us
  starting transfers between devices: 16.1 us -> 28.7 us
    all_gather x3 -> x0, blocking collectives: 46.1 us -> none  [local(): own_group = lax.all_gather(direction, 'sub', axis=0, tiled=True)]
    all_to_all x0 -> x3, starting transfers between devices: none -> 18.2 us  [local(): lax.all_to_all(jnp.stack([direction] * lax.axis_size('sub')), 'sub', 0, 0)]
    reduce_scatter x3, waiting for transfers between devices: 104 us -> 94.9 us  [local(): lax.psum_scatter(spread[:group_rows] + incoming, 'sub', scatter_dimension...]
  transfers between devices with their start and end apart: 9 -> 12, of which waited for: 8 -> 9; matrix products, arithmetic and copies ran while one was open for 1% -> 1% of each run, Pallas kernels for 0% -> 0%
where the time goes in v1:
time: 689 us; the launch traced here: 687 us
  blocking collectives  516 us (75%)
  waiting for transfers between devices  112 us (16%)
  starting transfers between devices  28.7 us (4%)
  between operations  14 us (2%)
    psum x3, blocking collectives, residual_sum(): return lax.psum(local_dots(residual_now, precond_now), ('dom', 'sub'))  305 us
    psum x2, blocking collectives, local(): curvature = lax.psum(local_dots(direction, image_vec), ('dom', 'sub'))  211 us
    reduce_scatter x3, waiting for transfers between devices, local(): lax.psum_scatter(spread[:group_rows] + incoming, 'sub', scatter_dimension...  94.9 us
    all_to_all x3, starting transfers between devices, local(): lax.all_to_all(jnp.stack([direction] * lax.axis_size('sub')), 'sub', 0, 0)  18.2 us
  transfers between devices with their start and end apart: 12, of which 9 were waited for; matrix products, arithmetic and copies ran while one was open for 1% of the time, Pallas kernels for 0%

profile of v1, /device:TPU:1, one launch (start us, length us, event | category | flops | bytes accessed | tf_op | source)
XLA Modules:
  0.0 687.1 jit_solution(12412002943891612536)
XLA Ops:
  8.6 10.3 %all-to-all-start = ((f32[8,2,16,128]{3,2,1,0:T(8,128)}), f32[8,2,16,128]{3,2,1,0:T(8,128)S(1)}, u32[]{:S(2)}, u32[]{:S(2)}) async-start(f32[8,2,16,128]{3,2,1,0:T(8,128)} %stack.6), calls=%async_computation | async-start | bytes 262144 | tf_op jit(solution)/shard_map/all_to_all | solution.py:43
  20.8 1.3 collective-permute-start.1
  22.4 1.8 all-to-all-done
  24.2 1.3 collective-permute-start
  26.2 4.0 collective-permute-done
  31.3 35.4 %reduce-scatter.4.cloned.1.call-done = f32[2,16,128]{2,1,0:T(8,128)} async-done(((f32[16,16,128]{2,1,0:T(8,128)}), f32[2,16,128]{2,1,0:T(8,128)}) %reduce-scatter.4.cloned.1.call-update) | async-done | bytes 16400 | tf_op jit(solution)/shard_map/reduce_scatter | solution.py:52
  66.7 0.8 multiply_reduce_fusion.4
  67.5 105.8 %all-reduce = (f32[16]{0:T(128)S(1)}, f32[16]{0:T(128)S(1)}) all-reduce(f32[16]{0:T(128)S(1)} %get-tuple-element.3, f32[16]{0:T(128)S(1)} %get-tuple-element.2), channel_id=1, replica_groups=mesh['dom'=64,'sub'=8] {'dom','sub'}, use_global_device_ids=true, to_apply=%region_1.2 | all-reduce | flops 32 | bytes 256 | tf_op jit(solution)/shard_map/psum | solution.py:31
  173.4 99.4 %psum.44 = f32[16]{0:T(128)S(1)} all-reduce(f32[16]{0:T(128)S(1)} %get-tuple-element.12), channel_id=1, replica_groups=mesh['dom'=64,'sub'=8] {'dom','sub'}, use_global_device_ids=true, to_apply=%region_6.7 | all-reduce | flops 16 | bytes 128 | tf_op jit(solution)/shard_map/psum | solution.py:31
  273.9 3.9 all-to-all-start.1
  278.4 2.7 collective-permute-start.3
  281.4 1.8 all-to-all-done.1
  283.2 1.3 collective-permute-start.2
  285.2 4.0 collective-permute-done.2
  290.3 29.8 %reduce-scatter.6.cloned.1.call-done = f32[2,16,128]{2,1,0:T(8,128)} async-done(((f32[16,16,128]{2,1,0:T(8,128)}), f32[2,16,128]{2,1,0:T(8,128)}) %reduce-scatter.6.cloned.1.call-update) | async-done | bytes 16400 | tf_op jit(solution)/shard_map/reduce_scatter | solution.py:52
  320.9 105.7 %psum.45 = f32[16]{0:T(128)S(1)} all-reduce(f32[16]{0:T(128)S(1)} %get-tuple-element.10), channel_id=1, replica_groups=mesh['dom'=64,'sub'=8] {'dom','sub'}, use_global_device_ids=true, to_apply=%region_9.10 | all-reduce | flops 16 | bytes 128 | tf_op jit(solution)/shard_map/psum | solution.py:56
  426.8 99.4 %psum.46 = f32[16]{0:T(128)S(1)} all-reduce(f32[16]{0:T(128)S(1)} %get-tuple-element.8), channel_id=1, replica_groups=mesh['dom'=64,'sub'=8] {'dom','sub'}, use_global_device_ids=true, to_apply=%region_11.12 | all-reduce | flops 16 | bytes 128 | tf_op jit(solution)/shard_map/psum | solution.py:31
  527.3 3.9 all-to-all-start.2
  531.7 2.7 collective-permute-start.5
  534.7 1.8 all-to-all-done.2
  536.5 1.3 collective-permute-start.4
  538.5 4.0 collective-permute-done.4
  543.6 29.8 %reduce-scatter.8.cloned.1.call-done = f32[2,16,128]{2,1,0:T(8,128)} async-done(((f32[16,16,128]{2,1,0:T(8,128)}), f32[2,16,128]{2,1,0:T(8,128)}) %reduce-scatter.8.cloned.1.call-update) | async-done | bytes 16400 | tf_op jit(solution)/shard_map/reduce_scatter | solution.py:52
  574.2 105.7 %psum.47 = f32[16]{0:T(128)S(1)} all-reduce(f32[16]{0:T(128)S(1)} %get-tuple-element.6), channel_id=1, replica_groups=mesh['dom'=64,'sub'=8] {'dom','sub'}, use_global_device_ids=true, to_apply=%region_14.15 | all-reduce | flops 16 | bytes 128 | tf_op jit(solution)/shard_map/psum | solution.py:56
  (69 shorter events, 15.3 us)
Async XLA Ops:
  7.2 11.8 %copy-start = (f32[2,4,128,128]{3,2,1,0:T(8,128)S(1)}, f32[2,4,128,128]{3,2,1,0:T(8,128)}, u32[]{:S(2)}) copy-start(f32[2,4,128,128]{3,2,1,0:T(8,128)} %param.8) | copy-start | bytes 1572868
  8.6 10.3 %copy-start.5 = (s32[2]{0:T(128)S(1)}, s32[2]{0:T(128)}, u32[]{:S(2)}) copy-start(s32[2]{0:T(128)} %param.10) | copy-start | bytes 28
  8.6 10.4 %copy-start.2 = (f32[2,16,128]{2,1,0:T(8,128)S(1)}, f32[2,16,128]{2,1,0:T(8,128)}, u32[]{:S(2)}) copy-start(f32[2,16,128]{2,1,0:T(8,128)} %param.6) | copy-start | bytes 49156
  8.6 15.6 %all-to-all-start = ((f32[8,2,16,128]{3,2,1,0:T(8,128)}), f32[8,2,16,128]{3,2,1,0:T(8,128)S(1)}, u32[]{:S(2)}, u32[]{:S(2)}) async-start(f32[8,2,16,128]{3,2,1,0:T(8,128)} %stack.6), calls=%async_computation | async-start | bytes 262144 | tf_op jit(solution)/shard_map/all_to_all | solution.py:43
  18.9 0.7 copy-start.3
  18.9 47.8 %reduce-scatter.4.cloned.1.call-start = ((), (), s32[]{:S(2)}) async-start(), calls=%async_computation.6 | async-start | bytes 147456 | tf_op jit(solution)/shard_map/reduce_scatter | solution.py:52
  19.6 0.7 copy-start.4
  20.7 1.4 copy-start.1
  20.8 4.7 collective-permute-start.1
  24.2 6.0 collective-permute-start
  273.9 9.2 %all-to-all-start.1 = ((f32[8,2,16,128]{3,2,1,0:T(8,128)}), f32[8,2,16,128]{3,2,1,0:T(8,128)S(1)}, u32[]{:S(2)}, u32[]{:S(2)}) async-start(f32[8,2,16,128]{3,2,1,0:T(8,128)} %stack.7), calls=%async_computation.2 | async-start | bytes 262144 | tf_op jit(solution)/shard_map/all_to_all | solution.py:43
  277.9 42.1 %reduce-scatter.6.cloned.1.call-start = ((), (), s32[]{:S(2)}) async-start(), calls=%async_computation.7 | async-start | bytes 147456 | tf_op jit(solution)/shard_map/reduce_scatter | solution.py:52
  278.4 6.1 collective-permute-start.3
  283.2 6.0 collective-permute-start.2
  527.3 9.2 %all-to-all-start.2 = ((f32[8,2,16,128]{3,2,1,0:T(8,128)}), f32[8,2,16,128]{3,2,1,0:T(8,128)S(1)}, u32[]{:S(2)}, u32[]{:S(2)}) async-start(f32[8,2,16,128]{3,2,1,0:T(8,128)} %stack.8), calls=%async_computation.4 | async-start | bytes 262144 | tf_op jit(solution)/shard_map/all_to_all | solution.py:43
  531.2 42.2 %reduce-scatter.8.cloned.1.call-start = ((), (), s32[]{:S(2)}) async-start(), calls=%async_computation.8 | async-start | bytes 147456 | tf_op jit(solution)/shard_map/reduce_scatter | solution.py:52
  531.7 6.1 collective-permute-start.5
  536.5 6.0 collective-permute-start.4
Sparse Core Ops, SparseCore 0:
  26.3 40.2 reduce-scatter.3
  285.3 34.6 reduce-scatter.5
  538.6 34.6 reduce-scatter.7

commit v2 on v0

--- a/solution.py
+++ b/solution.py
@@ -51,7 +51,7 @@
             spread[:group_rows] + incoming, "sub", scatter_dimension=0, tiled=True
         )
         image_vec = own_part + forward + back_own
-        curvature = lax.psum(local_dots(direction, image_vec), ("dom", "sub"))
+        curvature = lax.psum(lax.psum(local_dots(direction, image_vec), "dom"), "sub")
         step_size = precond_dot / curvature
         solution_field = solution_field + step_size[None, :, None] * direction
         residual = residual - step_size[None, :, None] * image_vec

time: 717 us -> 966 us (1.35)
  blocking collectives: 562 us -> 818 us
    psum x2 -> x6, blocking collectives: 212 us -> 468 us  [the longest x3 343 us: local(): lax.psum(local_dots(direction, image_vec), 'dom')]
where the time goes in v2:
time: 966 us; the launch traced here: 965 us
  blocking collectives  818 us (85%)
  waiting for transfers between devices  103 us (11%)
  starting transfers between devices  16.7 us (2%)
  between operations  14 us (1%)
    psum x3, blocking collectives, local(): lax.psum(local_dots(direction, image_vec), 'dom')  343 us
    psum x3, blocking collectives, residual_sum(): return lax.psum(local_dots(residual_now, precond_now), ('dom', 'sub'))  303 us
    psum x3, blocking collectives, local(): lax.psum(lax.psum(local_dots(direction, image_vec), 'dom'), 'sub')  125 us
    reduce_scatter x3, waiting for transfers between devices, local(): lax.psum_scatter(spread[:group_rows] + incoming, 'sub', scatter_dimension...  96.8 us
    all_gather x3, blocking collectives, local(): own_group = lax.all_gather(direction, 'sub', axis=0, tiled=True)  46.1 us
  transfers between devices with their start and end apart: 9, of which 8 were waited for; matrix products, arithmetic and copies ran while one was open for 1% of the time, Pallas kernels for 0%

profile of v2, /device:TPU:1, one launch (start us, length us, event | category | flops | bytes accessed | tf_op | source)
XLA Modules:
  0.0 964.7 jit_solution(6920247303215485182)
XLA Ops:
  8.0 19.6 %all_gather.9 = f32[16,16,128]{2,1,0:T(8,128)S(1)} all-gather(f32[2,16,128]{2,1,0:T(8,128)S(1)} %broadcast_divide_fusion), channel_id=1, replica_groups=mesh['dom'=64,'sub'=8] {'sub'}, dimensions={0}, use_global_device_ids=true | all-gather | bytes 147456 | tf_op jit(solution)/shard_map/all_gather | solution.py:42
  27.6 1.4 collective-permute-start
  30.3 4.0 collective-permute-start.1
  35.0 1.7 collective-permute-done.1
  38.2 37.2 %reduce-scatter.4.cloned.1.call-done = f32[2,16,128]{2,1,0:T(8,128)} async-done(((f32[16,16,128]{2,1,0:T(8,128)}), f32[2,16,128]{2,1,0:T(8,128)}) %reduce-scatter.4.cloned.1.call-update) | async-done | bytes 16400 | tf_op jit(solution)/shard_map/reduce_scatter | solution.py:50
  76.2 105.8 %psum.63 = f32[16]{0:T(128)S(1)} all-reduce(f32[16]{0:T(128)S(1)} %get-tuple-element.3), channel_id=1, replica_groups=mesh['dom'=64,'sub'=8] {'dom','sub'}, use_global_device_ids=true, to_apply=%region_1.2 | all-reduce | flops 16 | bytes 128 | tf_op jit(solution)/shard_map/psum | solution.py:31
  182.0 112.1 %psum.64 = f32[16]{0:T(128)S(1)} all-reduce(f32[16]{0:T(128)S(1)} %get-tuple-element.2), channel_id=1, replica_groups=mesh['dom'=64,'sub'=8] {'dom'}, use_global_device_ids=true, to_apply=%region_4.5 | all-reduce | flops 16 | bytes 128 | tf_op jit(solution)/shard_map/psum | solution.py:54
  294.1 39.9 %psum.65 = f32[16]{0:T(128)S(1)} all-reduce(f32[16]{0:T(128)S(1)} %psum.64), channel_id=1, replica_groups=mesh['dom'=64,'sub'=8] {'sub'}, use_global_device_ids=true, to_apply=%region_5.6 | all-reduce | flops 16 | bytes 128 | tf_op jit(solution)/shard_map/psum | solution.py:54
  334.2 98.7 %psum.66 = f32[16]{0:T(128)S(1)} all-reduce(f32[16]{0:T(128)S(1)} %get-tuple-element.10), channel_id=1, replica_groups=mesh['dom'=64,'sub'=8] {'dom','sub'}, use_global_device_ids=true, to_apply=%region_7.8 | all-reduce | flops 16 | bytes 128 | tf_op jit(solution)/shard_map/psum | solution.py:31
  433.0 13.2 %all_gather.10 = f32[16,16,128]{2,1,0:T(8,128)S(1)} all-gather(f32[2,16,128]{2,1,0:T(8,128)S(1)} %multiply_add_fusion.2), channel_id=1, replica_groups=mesh['dom'=64,'sub'=8] {'sub'}, dimensions={0}, use_global_device_ids=true | all-gather | bytes 147456 | tf_op jit(solution)/shard_map/all_gather | solution.py:42
  446.6 1.3 collective-permute-start.2
  448.4 4.3 collective-permute-start.3
  453.0 1.1 collective-permute-done.2
  456.9 29.7 %reduce-scatter.6.cloned.1.call-done = f32[2,16,128]{2,1,0:T(8,128)} async-done(((f32[16,16,128]{2,1,0:T(8,128)}), f32[2,16,128]{2,1,0:T(8,128)}) %reduce-scatter.6.cloned.1.call-update) | async-done | bytes 16400 | tf_op jit(solution)/shard_map/reduce_scatter | solution.py:50
  487.5 115.7 %psum.67 = f32[16]{0:T(128)S(1)} all-reduce(f32[16]{0:T(128)S(1)} %get-tuple-element.8), channel_id=1, replica_groups=mesh['dom'=64,'sub'=8] {'dom'}, use_global_device_ids=true, to_apply=%region_10.11 | all-reduce | flops 16 | bytes 128 | tf_op jit(solution)/shard_map/psum | solution.py:54
  603.2 42.5 %psum.68 = f32[16]{0:T(128)S(1)} all-reduce(f32[16]{0:T(128)S(1)} %psum.67), channel_id=1, replica_groups=mesh['dom'=64,'sub'=8] {'sub'}, use_global_device_ids=true, to_apply=%region_11.12 | all-reduce | flops 16 | bytes 128 | tf_op jit(solution)/shard_map/psum | solution.py:54
  646.0 98.7 %psum.69 = f32[16]{0:T(128)S(1)} all-reduce(f32[16]{0:T(128)S(1)} %get-tuple-element.6), channel_id=1, replica_groups=mesh['dom'=64,'sub'=8] {'dom','sub'}, use_global_device_ids=true, to_apply=%region_13.14 | all-reduce | flops 16 | bytes 128 | tf_op jit(solution)/shard_map/psum | solution.py:31
  744.7 13.2 %all_gather.11 = f32[16,16,128]{2,1,0:T(8,128)S(1)} all-gather(f32[2,16,128]{2,1,0:T(8,128)S(1)} %multiply_add_fusion.1), channel_id=1, replica_groups=mesh['dom'=64,'sub'=8] {'sub'}, dimensions={0}, use_global_device_ids=true | all-gather | bytes 147456 | tf_op jit(solution)/shard_map/all_gather | solution.py:42
  758.3 1.3 collective-permute-start.4
  760.1 4.3 collective-permute-start.5
  764.7 1.1 collective-permute-done.4
  768.6 29.9 %reduce-scatter.8.cloned.1.call-done = f32[2,16,128]{2,1,0:T(8,128)} async-done(((f32[16,16,128]{2,1,0:T(8,128)}), f32[2,16,128]{2,1,0:T(8,128)}) %reduce-scatter.8.cloned.1.call-update) | async-done | bytes 16400 | tf_op jit(solution)/shard_map/reduce_scatter | solution.py:50
  799.3 115.6 %psum.70 = f32[16]{0:T(128)S(1)} all-reduce(f32[16]{0:T(128)S(1)} %get-tuple-element.4), channel_id=1, replica_groups=mesh['dom'=64,'sub'=8] {'dom'}, use_global_device_ids=true, to_apply=%region_16.17 | all-reduce | flops 16 | bytes 128 | tf_op jit(solution)/shard_map/psum | solution.py:54
  915.0 42.5 %psum.71 = f32[16]{0:T(128)S(1)} all-reduce(f32[16]{0:T(128)S(1)} %psum.70), channel_id=1, replica_groups=mesh['dom'=64,'sub'=8] {'sub'}, use_global_device_ids=true, to_apply=%region_17.18 | all-reduce | flops 16 | bytes 128 | tf_op jit(solution)/shard_map/psum | solution.py:54
  (67 shorter events, 15.8 us)
Async XLA Ops:
  7.2 21.9 %copy-start = (f32[2,4,128,128]{3,2,1,0:T(8,128)S(1)}, f32[2,4,128,128]{3,2,1,0:T(8,128)}, u32[]{:S(2)}) copy-start(f32[2,4,128,128]{3,2,1,0:T(8,128)} %param.8) | copy-start | bytes 1572868
  7.2 68.2 %reduce-scatter.4.cloned.1.call-start = ((), (), s32[]{:S(2)}) async-start(), calls=%async_computation.3 | async-start | bytes 147456 | tf_op jit(solution)/shard_map/reduce_scatter | solution.py:50
  8.0 21.0 %copy-start.5 = (s32[2]{0:T(128)S(1)}, s32[2]{0:T(128)}, u32[]{:S(2)}) copy-start(s32[2]{0:T(128)} %param.10) | copy-start | bytes 28
  8.0 21.1 %copy-start.2 = (f32[2,16,128]{2,1,0:T(8,128)S(1)}, f32[2,16,128]{2,1,0:T(8,128)}, u32[]{:S(2)}) copy-start(f32[2,16,128]{2,1,0:T(8,128)} %param.6) | copy-start | bytes 49156
  27.6 1.5 copy-start.3
  27.6 7.0 collective-permute-start
  29.1 0.7 copy-start.4
  30.2 4.1 copy-start.1
  30.3 6.4 collective-permute-start.1
  37.4 449.3 %reduce-scatter.6.cloned.1.call-start = ((), (), s32[]{:S(2)}) async-start(), calls=%async_computation.4 | async-start | bytes 147456 | tf_op jit(solution)/shard_map/reduce_scatter | solution.py:50
  446.6 7.5 collective-permute-start.2
  448.4 7.0 collective-permute-start.3
  456.1 342.4 %reduce-scatter.8.cloned.1.call-start = ((), (), s32[]{:S(2)}) async-start(), calls=%async_computation.5 | async-start | bytes 147456 | tf_op jit(solution)/shard_map/reduce_scatter | solution.py:50
  758.3 7.5 collective-permute-start.4
  760.1 7.0 collective-permute-start.5
Sparse Core Ops, SparseCore 0:
  37.5 37.8 reduce-scatter.3
  456.3 30.3 reduce-scatter.5
  768.0 30.4 reduce-scatter.7
